TPU v7x, 32 devices: a whole 2x2x4 slice. The times are simulated.
32 devices in a mesh: group: 2 (over y), wide: 4 (over z), narrow: 4 (over x, core).
Axes of the slice: x: 2, y: 2, z: 4, core: 2. Of those that a mesh axis runs over, the one named last changes fastest.
Arguments:
- field: bfloat16 [32768, 512], P(('group', 'wide', 'narrow')), parts along dimension 0, may hold values from -24 to 24
- w_embed: bfloat16 [512, 512], replicated, may hold values from -0.25 to 0.25
- embed_bias: float32 [512], replicated, may hold values from -4 to 4
- w_query: bfloat16 [512, 512], replicated, may hold values from -0.25 to 0.25
- w_key: bfloat16 [512, 512], replicated, may hold values from -0.25 to 0.25
- w_value: bfloat16 [512, 512], replicated, may hold values from -0.25 to 0.25
- w_out: bfloat16 [512, 512], replicated, may hold values from -0.25 to 0.25
- latents: bfloat16 [512, 512], replicated, may hold values from -120 to 120
- out_gain: float32 [512], replicated, may hold values from 0.5 to 1.5
Outputs:
- encoded: bfloat16 [1024, 512], P('group'), parts along dimension 0
There are 2 independent parts, one for each index of `group`. A program takes and returns all parts, laid end to end along the dimension named above; an argument that names none is the same for every part. Nothing has to cross between parts.
All inputs are finite; a program needn't handle non-finite values.
Results may differ from a plain program's by a relative error of at most 0.012.
The roundings to bfloat16 on the way count: a program that leaves them out, or rounds other values in their place, can miss the bound.
Values may be sent and summed in bfloat16 or wider, within the bound.
A program may use at most 64 MiB of HBM per device.

v0:
```python
import jax
import jax.numpy as jnp
from jax import lax
from jax.sharding import PartitionSpec as P

HEADS = 8


def finish(numer, denom, latent_rows, w_out, out_gain, heads):
    count, width = numer.shape
    ratio = numer.reshape(count, heads, width // heads) / denom[:, :, None]
    attended = ratio.reshape(count, width).astype(jnp.bfloat16)
    mixed = latent_rows.astype(jnp.float32) + jnp.dot(
        attended, w_out, preferred_element_type=jnp.float32
    )
    center = mixed - jnp.mean(mixed, axis=1, keepdims=True)
    spread = jnp.mean(center * center, axis=1, keepdims=True)
    return (center * lax.rsqrt(spread + 1e-05) * out_gain).astype(jnp.bfloat16)


def body(field, w_embed, embed_bias, w_query, w_key, w_value, w_out, latents, out_gain):
    tok_rows = field.shape[0]
    lat_rows, width = latents.shape
    heads = HEADS
    head_dim = width // heads
    emb = (jnp.dot(field, w_embed, preferred_element_type=jnp.float32) + embed_bias).astype(
        jnp.bfloat16
    )
    keys = jnp.dot(emb, w_key, preferred_element_type=jnp.float32).astype(jnp.bfloat16)
    values = jnp.dot(emb, w_value, preferred_element_type=jnp.float32).astype(jnp.bfloat16)
    queries = (
        jnp.dot(latents, w_query, preferred_element_type=jnp.float32) * head_dim ** (-0.5)
    ).astype(jnp.bfloat16)
    query_heads = queries.reshape(lat_rows, heads, head_dim)
    block = min(512, tok_rows)
    blocks = tok_rows // block

    def block_scores(index):
        key_block = keys[index * block : (index + 1) * block].reshape(block, heads, head_dim)
        return jnp.einsum(
            "lhe,the->lht", query_heads, key_block, preferred_element_type=jnp.float32
        )

    def scores_of(index):
        return block_scores(index)

    local_top = jnp.max(scores_of(0), axis=2)
    index = 1
    local_top = jnp.maximum(local_top, jnp.max(scores_of(index), axis=2))
    top = lax.pmax(local_top, ("wide", "narrow"))
    denom = jnp.zeros((lat_rows, heads), jnp.float32)
    numer = jnp.zeros((lat_rows, heads, head_dim), jnp.float32)
    for index in range(blocks):
        expo = jnp.exp(scores_of(index) - top[:, :, None])
        denom = denom + jnp.sum(expo, axis=2)
        value_block = values[index * block : (index + 1) * block].reshape(block, heads, head_dim)
        numer = numer + jnp.einsum(
            "lht,the->lhe",
            expo.astype(jnp.bfloat16),
            value_block,
            preferred_element_type=jnp.float32,
        )
    numer = numer.reshape(lat_rows, width)
    numer_all, denom_all = lax.psum((numer, denom), ("wide", "narrow"))
    return finish(numer_all, denom_all, latents, w_out, out_gain, heads)


def solution(mesh):
    placed = (P(("group", "wide", "narrow"), None), P(), P(), P(), P(), P(), P(), P(), P())
    return jax.shard_map(
        body, mesh=mesh, in_specs=placed, out_specs=P("group", None), check_vma=False
    )
```

profile of v0, /device:TPU:0, one launch (start us, length us, event | category | flops | bytes accessed | tf_op | source)
XLA Modules:
  0.0 196.1 jit_solution(12706030199588957566)
XLA Ops:
  6.5 0.0 copy-start
  6.5 0.0 copy-start.4
  6.5 0.0 copy-start.1
  6.5 0.0 all-reduce.2.cloned.1.call-start
  6.5 1.2 copy-done
  7.8 1.7 add_convert_fusion
  9.5 1.8 convolution_convert_fusion
  11.3 0.1 fusion.18
  11.4 0.0 copy-done.4
  11.4 0.0 copy-done.1
  11.4 0.5 fusion.15
  11.9 0.0 copy-start.5
  11.9 4.5 %bitcast_reduce_fusion.1 = (f32[512,8]{0,1:T(8,128)S(1)}, f32[8,512,512]{2,1,0:T(8,128)}) fusion(bf16[512,8,64]{0,2,1:T(8,128)(2,1)S(1)} %bitcast.54, bf16[512,8,64]{0,2,1:T(8,128)(2,1)S(1)} %bitcast.51), kind=kOutput, calls=%fused_computation.4 | convolution fusion | flops 270528512 | bytes 9453568 | tf_op jit(solution)/shard_map/lhe,the->lht/dot_general | solution.py:40
  16.4 4.5 %bitcast_reduce_fusion = (f32[512,8]{0,1:T(8,128)S(1)}, f32[8,512,512]{2,1,0:T(8,128)}) fusion(bf16[512,8,64]{0,2,1:T(8,128)(2,1)S(1)} %bitcast.53, bf16[512,8,64]{0,2,1:T(8,128)(2,1)S(1)} %bitcast.52), kind=kOutput, calls=%fused_computation.1 | convolution fusion | flops 270528512 | bytes 9453568 | tf_op jit(solution)/shard_map/lhe,the->lht/dot_general | solution.py:40
  20.9 62.9 %pmax.7 = f32[512,8]{0,1:T(8,128)S(1)} all-reduce(f32[512,8]{0,1:T(8,128)S(1)} %max.5), channel_id=1, replica_groups=mesh['group'=2,'wide'=4,'narrow'=4] {'wide','narrow'}, use_global_device_ids=true, to_apply=%region_2.0 | all-reduce | flops 4096 | bytes 32768 | tf_op jit(solution)/shard_map/pmax | solution.py:50
  83.9 0.0 copy-done.5
  83.9 0.8 convolution_convert_fusion.1
  84.6 0.1 fusion.17
  84.7 4.8 %fusion.6 = f32[8,64,512]{2,1,0:T(8,128)S(1)} fusion(bf16[512,8,64]{0,2,1:T(8,128)(2,1)S(1)} %bitcast.55, f32[8,512,512]{2,1,0:T(8,128)} %get-tuple-element.14, f32[512,8]{0,1:T(8,128)S(1)} %pmax.7), kind=kOutput, calls=%fused_computation.10 | convolution fusion | flops 272629760 | bytes 9977856 | tf_op jit(solution)/shard_map/lht,the->lhe/dot_general | solution.py:57
  89.5 5.8 %fusion.12 = f32[8,64,512]{2,1,0:T(8,128)} fusion(f32[8,64,512]{2,1,0:T(8,128)S(1)} %fusion.6, bf16[512,8,64]{0,2,1:T(8,128)(2,1)S(1)} %bitcast.56, f32[8,512,512]{2,1,0:T(8,128)} %get-tuple-element.12, f32[512,8]{0,1:T(8,128)S(1)} %pmax.7), kind=kOutput, calls=%fused_computation.19 | convolution fusion | flops 272891904 | bytes 11026432 | tf_op jit(solution)/shard_map/lht,the->lhe/dot_general | solution.py:57
  95.3 0.0 all-reduce.2.cloned.1.call-update
  95.4 0.2 copy.10
  95.6 0.0 copy-start.2
  95.6 0.0 copy-start.3
  95.6 7.2 %fusion.4 = (f32[512,8]{0,1:T(8,128)S(1)}, f32[512,8]{0,1:T(8,128)S(1)}) fusion(f32[8,512,512]{2,1,0:T(8,128)} %get-tuple-element.14, f32[512,8]{0,1:T(8,128)S(1)} %pmax.7, f32[8,512,512]{2,1,0:T(8,128)} %get-tuple-element.12), kind=kLoop, calls=%fused_computation.8 | loop fusion | flops 8380416 | bytes 16826368 | tf_op jit(solution)/shard_map/reduce_sum | solution.py:55
  102.8 57.9 %psum.15 = f32[512,8]{0,1:T(8,128)S(1)} all-reduce(f32[512,8]{0,1:T(8,128)S(1)} %add.39), channel_id=1, replica_groups=mesh['group'=2,'wide'=4,'narrow'=4] {'wide','narrow'}, use_global_device_ids=true, to_apply=%region_6.0 | all-reduce | flops 4096 | bytes 32768 | tf_op jit(solution)/shard_map/psum | solution.py:64
  160.7 25.4 %all-reduce.2.cloned.1.call-done = f32[512,512]{0,1:T(8,128)} async-done(((f32[512,512]{0,1:T(8,128)}), f32[512,512]{0,1:T(8,128)}) %all-reduce.2.cloned.1.call-update) | async-done | bytes 1048592 | tf_op jit(solution)/shard_map/psum | solution.py:64
  186.1 1.3 fusion.16
  187.4 0.0 copy-done.2
  187.4 0.5 fusion.19
  187.9 0.2 multiply_reduce_fusion
  188.1 0.0 copy-done.3
  188.1 0.2 multiply_convert_fusion
  188.3 1.0 copy.13
  (4 shorter events, 0.0 us)
Async XLA Ops:
  6.5 1.2 copy-start
  6.5 4.9 %copy-start.4 = (bf16[512,512]{1,0:T(8,128)(2,1)S(1)}, bf16[512,512]{1,0:T(8,128)(2,1)}, u32[]{:S(2)}) copy-start(bf16[512,512]{1,0:T(8,128)(2,1)} %param.12) | copy-start | bytes 1572868
  6.5 4.9 %copy-start.1 = (bf16[512,512]{1,0:T(8,128)(2,1)S(1)}, bf16[512,512]{1,0:T(8,128)(2,1)}, u32[]{:S(2)}) copy-start(bf16[512,512]{1,0:T(8,128)(2,1)} %param.16) | copy-start | bytes 1572868
  6.5 179.5 %all-reduce.2.cloned.1.call-start = ((), (), s32[]{:S(2)}) async-start(), calls=%async_computation | async-start | bytes 2097152 | tf_op jit(solution)/shard_map/psum | solution.py:64
  11.9 72.0 %copy-start.5 = (bf16[512,512]{1,0:T(8,128)(2,1)S(1)}, bf16[512,512]{1,0:T(8,128)(2,1)}, u32[]{:S(2)}) copy-start(bf16[512,512]{1,0:T(8,128)(2,1)} %param.14) | copy-start | bytes 1572868
  95.6 91.8 %copy-start.2 = (bf16[512,512]{1,0:T(8,128)(2,1)S(1)}, bf16[512,512]{1,0:T(8,128)(2,1)}, u32[]{:S(2)}) copy-start(bf16[512,512]{1,0:T(8,128)(2,1)} %param.15) | copy-start | bytes 1572868
  95.6 92.5 %copy-start.3 = (f32[512]{0:T(512)S(1)}, f32[512]{0:T(512)}, u32[]{:S(2)}) copy-start(f32[512]{0:T(512)} %param.17) | copy-start | bytes 6148
Sparse Core Ops, SparseCore 0:
  95.5 90.5 all-reduce.1
where the time goes:
time: 196 us
  blocking collectives  121 us (62%)
  waiting for transfers between devices  25.4 us (13%)
  matrix products  24.9 us (13%)
  between operations  13.5 us (7%)
  other arithmetic  8.88 us (5%)
  local copies, waits for them, and re-layouts  2.6 us (1%)
    pmax x1, blocking collectives, body(): top = lax.pmax(local_top, ('wide', 'narrow'))  62.9 us
    psum x1, blocking collectives, body(): numer_all, denom_all = lax.psum((numer, denom), ('wide', 'narrow'))  57.9 us
    psum x1, waiting for transfers between devices, body(): numer_all, denom_all = lax.psum((numer, denom), ('wide', 'narrow'))  25.4 us
    dot_general x2, matrix products, body(): jnp.einsum('lht,the->lhe', expo.astype(jnp.bfloat16), value_block, prefer...  10.6 us
    dot_general x2, matrix products, block_scores(): jnp.einsum('lhe,the->lht', query_heads, key_block, preferred_element_type...  9.02 us
    reduce_sum x1, other arithmetic, body(): denom = denom + jnp.sum(expo, axis=2)  7.19 us
  transfers between devices with their start and end apart: 1, of which 1 were waited for; matrix products, arithmetic and copies ran while one was open for 4% of the time, Pallas kernels for 0%

commit v1 on v0

v1 whole, which is shorter than its diff:
```python
import functools

import jax
import jax.numpy as jnp
from jax import lax
from jax.experimental import pallas as pl
from jax.experimental.pallas import tpu as pltpu
from jax.sharding import PartitionSpec as P

HEADS = 8
F32 = jnp.float32
BF16 = jnp.bfloat16
MESH = pl.DeviceIdType.MESH


def finish(numer, denom, latent_rows, w_out, out_gain, heads):
    count, width = numer.shape
    ratio = numer.reshape(count, heads, width // heads) / denom[:, :, None]
    attended = ratio.reshape(count, width).astype(BF16)
    mixed = latent_rows.astype(F32) + jnp.dot(attended, w_out, preferred_element_type=F32)
    center = mixed - jnp.mean(mixed, axis=1, keepdims=True)
    spread = jnp.mean(center * center, axis=1, keepdims=True)
    return (center * lax.rsqrt(spread + 1e-05) * out_gain).astype(BF16)


def plain_body(field, w_embed, embed_bias, w_query, w_key, w_value, w_out, latents, out_gain):
    tok_rows = field.shape[0]
    lat_rows, width = latents.shape
    heads = HEADS
    head_dim = width // heads
    emb = (jnp.dot(field, w_embed, preferred_element_type=F32) + embed_bias).astype(BF16)
    keys = jnp.dot(emb, w_key, preferred_element_type=F32).astype(BF16)
    values = jnp.dot(emb, w_value, preferred_element_type=F32).astype(BF16)
    queries = (jnp.dot(latents, w_query, preferred_element_type=F32) * head_dim ** (-0.5)).astype(
        BF16
    )
    query_heads = queries.reshape(lat_rows, heads, head_dim)
    key_heads = keys.reshape(tok_rows, heads, head_dim)
    value_heads = values.reshape(tok_rows, heads, head_dim)
    scores = jnp.einsum("lhe,the->hlt", query_heads, key_heads, preferred_element_type=F32)
    top = lax.pmax(jnp.max(scores, axis=2), ("wide", "narrow"))
    expo = jnp.exp(scores - top[:, :, None])
    denom = jnp.sum(expo, axis=2).T
    numer = jnp.einsum(
        "hlt,the->lhe", expo.astype(BF16), value_heads, preferred_element_type=F32
    ).reshape(lat_rows, width)
    numer, denom = lax.psum((numer, denom), ("wide", "narrow"))
    return finish(numer, denom, latents, w_out, out_gain, heads)


TOP_COLS = 24
STAT_COLS = 40


def lanes(shape):
    return lax.broadcasted_iota(jnp.int32, shape, len(shape) - 1)


def encode(stat):
    high = stat.astype(BF16).astype(F32)
    rest = stat - high
    middle = rest.astype(BF16).astype(F32)
    low = rest - middle
    group = lanes(stat.shape) // 8
    part = jnp.where((group == 0) | (group == 3), high, jnp.where(group == 2, low, middle))
    return part.astype(BF16)


def make_spread(spread, width, heads):
    head_dim = width // heads
    row = lax.broadcasted_iota(jnp.int32, (128, width), 0)
    col = lanes((128, width))
    same = (row % 8) == (col // head_dim)
    spread[:, :width] = jnp.where(same & (row < TOP_COLS), 1.0, 0.0).astype(BF16)
    denom = same & (row >= TOP_COLS) & (row < STAT_COLS)
    spread[:, width + 256 :] = jnp.where(denom, 1.0, 0.0).astype(BF16)
    row = lax.broadcasted_iota(jnp.int32, (128, 128), 0)
    col = lanes((128, 128))
    same = ((row % 8) == (col % 8)) & (col < STAT_COLS)
    spread[:, width : width + 128] = jnp.where(same & (row < TOP_COLS), 1.0, 0.0).astype(BF16)
    denom = same & (row >= TOP_COLS) & (row < STAT_COLS)
    spread[:, width + 128 : width + 256] = jnp.where(denom, 1.0, 0.0).astype(BF16)


def merge(numers, stats, spread, width):
    full = [jnp.dot(s, spread[:, : width + 256], preferred_element_type=F32) for s in stats]
    top = functools.reduce(jnp.maximum, [f[:, : width + 128] for f in full])
    scale = [jnp.exp(f[:, : width + 128] - top) for f in full]
    numer = sum(n.astype(F32) * s[:, :width] for n, s in zip(numers, scale))
    denom = sum(f[:, width + 128 :] * s[:, width:] for f, s in zip(full, scale))
    stat = jnp.where(lanes(denom.shape) < TOP_COLS, top[:, width:], denom)
    return numer, encode(stat)


def merge_ratio(numers, stats, spread, width):
    full = [jnp.dot(s, spread[...], preferred_element_type=F32) for s in stats]
    top = functools.reduce(jnp.maximum, [f[:, :width] for f in full])
    scale = [jnp.exp(f[:, :width] - top) for f in full]
    numer = sum(n.astype(F32) * s for n, s in zip(numers, scale))
    denom = sum(f[:, width + 256 :] * s for f, s in zip(full, scale))
    return numer / denom


def kernel(
    deep,
    field,
    w_embed,
    embed_bias,
    w_query,
    w_key,
    w_value,
    w_out,
    latents,
    out_gain,
    out,
    queries,
    keys_t,
    vaug,
    spread,
    own_numer,
    own_stat,
    core_out,
    core_in,
    x_out,
    x_in,
    z_out,
    z_in,
    send,
    recv,
):
    tokens = field.shape[0]
    rows, width = latents.shape
    heads = HEADS
    head_dim = width // heads
    half, quarter, piece = rows // 2, rows // 4, rows // 4 // deep

    group, w, n = lax.axis_index("group"), lax.axis_index("wide"), lax.axis_index("narrow")
    c, x = lax.rem(n, 2), n // 2
    sibling = (group, w, x * 2 + 1 - c)
    across = (group, w, (1 - x) * 2 + c)
    along = [None] + [(group, lax.rem(w + k, deep), n) for k in range(1, deep)]

    barrier = pltpu.get_barrier_semaphore()
    for other in [sibling, across] + along[1:]:
        pl.semaphore_signal(barrier, inc=1, device_id=other, device_id_type=MESH)

    def copy(index, source, target, device):
        return pltpu.make_async_remote_copy(
            src_ref=source,
            dst_ref=target,
            send_sem=send.at[index],
            recv_sem=recv.at[index],
            device_id=device,
            device_id_type=MESH,
        )

    make_spread(spread, width, heads)
    queries[...] = (
        jnp.dot(latents[...], w_query[...], preferred_element_type=F32) * head_dim ** (-0.5)
    ).astype(BF16)

    chunk = 256

    @pl.loop(0, tokens // chunk)
    def project(step):
        at = pl.multiple_of(step * chunk, chunk)
        emb = (
            jnp.dot(field[pl.ds(at, chunk), :], w_embed[...], preferred_element_type=F32)
            + embed_bias[...]
        ).astype(BF16)
        keys = jnp.dot(emb, w_key[...], preferred_element_type=F32).astype(BF16)
        keys_t[:, pl.ds(at, chunk)] = keys.T
        values = jnp.dot(emb, w_value[...], preferred_element_type=F32)
        lane = lanes((chunk, 128))
        for pair in range(heads // 2):
            both = values[:, pair * 128 : pair * 128 + 128]
            for side in range(2):
                mine = (lane // head_dim) == side
                ones = (lane % 8 == pair * 2 + side) & (lane >= TOP_COLS) & (lane < STAT_COLS)
                target = pl.ds(side * tokens + at, chunk)
                vaug[pair, target, :128] = jnp.where(mine, both, 0.0).astype(BF16)
                vaug[pair, target, 128:] = jnp.where(ones, 1.0, 0.0).astype(BF16)

    def attend(start, numer_out, stat_out):
        lane = lanes((half, 128))
        stat = jnp.zeros((half, 128), F32)
        for pair in range(heads // 2):
            cols = slice(pair * 128, pair * 128 + 128)
            query = queries[pl.ds(start, half), cols]
            probs = []
            for side in range(2):
                one = jnp.where((lane // head_dim) == side, query.astype(F32), 0.0).astype(BF16)
                scores = jnp.dot(one, keys_t[cols, :], preferred_element_type=F32)
                top = jnp.max(scores, axis=1, keepdims=True)
                probs.append(jnp.exp(scores - top).astype(BF16))
                here = (lane % 8 == pair * 2 + side) & (lane < TOP_COLS)
                stat = jnp.where(here, top, stat)
            result = jnp.dot(
                jnp.concatenate(probs, axis=1), vaug[pair], preferred_element_type=F32
            )
            numer_out[:, cols] = result[:, :128].astype(numer_out.dtype)
            stat = stat + result[:, 128:]
        stat_out[...] = encode(stat)

    attend(
        pl.multiple_of((1 - c) * half, half), core_out.at[:, :width], core_out.at[:, width:]
    )
    pl.semaphore_wait(barrier, 1 + deep)
    sent = [copy(0, core_out, core_in, sibling)]
    sent[0].start()
    attend(pl.multiple_of(c * half, half), own_numer, own_stat)
    sent[0].wait_recv()

    def chip_sum(at):
        at = pl.multiple_of(at, piece)
        return merge(
            [own_numer[pl.ds(at, piece), :], core_in[pl.ds(at, piece), :width]],
            [own_stat[pl.ds(at, piece), :], core_in[pl.ds(at, piece), width:]],
            spread,
            width,
        )

    order = list(range(1, deep)) + [0]
    index = 1
    x_copies = {}
    for k in order:
        block = lax.rem(w + k, deep)
        numer, stat = chip_sum((1 - x) * quarter + block * piece)
        x_out[k, :, :width] = numer.astype(BF16)
        x_out[k, :, width:] = stat
        x_copies[k] = copy(index, x_out.at[k], x_in.at[k], across)
        x_copies[k].start()
        index += 1
    mine = {}
    for k in order:
        block = lax.rem(w + k, deep)
        mine[k] = chip_sum(x * quarter + block * piece)
    z_copies = {}
    for k in order:
        x_copies[k].wait_recv()
        numer, stat = merge(
            [mine[k][0], x_in[k, :, :width]], [mine[k][1], x_in[k, :, width:]], spread, width
        )
        if k:
            z_out[k, :, :width] = numer.astype(BF16)
            z_out[k, :, width:] = stat
            z_copies[k] = copy(index, z_out.at[k], z_in.at[k], along[k])
            z_copies[k].start()
            index += 1
    numers, stats = [numer], [stat]
    for k in order[:-1]:
        z_copies[k].wait_recv()
        numers.append(z_in[k, :, :width])
        stats.append(z_in[k, :, width:])
    attended = merge_ratio(numers, stats, spread, width).astype(BF16)

    def place(core, column, slab):
        return pl.ds(pl.multiple_of(core * half + column * quarter + slab * piece, piece), piece)

    own = place(c, x, w)
    mixed = latents[own, :].astype(F32) + jnp.dot(
        attended, w_out[...], preferred_element_type=F32
    )
    center = mixed - jnp.mean(mixed, axis=1, keepdims=True)
    variance = jnp.mean(center * center, axis=1, keepdims=True)
    out[own, :] = (center * lax.rsqrt(variance + 1e-05) * out_gain[...]).astype(BF16)

    z_gather, x_gather, s_gather = {}, {}, {}

    def gather(store, key, at, device):
        nonlocal index
        store[key] = copy(index, out.at[at], out.at[at], device)
        store[key].start()
        index += 1

    for k in range(1, deep):
        gather(z_gather, k, own, along[k])
    gather(x_gather, 0, own, across)
    gather(s_gather, 0, own, sibling)
    for k in range(1, deep):
        z_gather[k].wait_recv()
        came = place(c, x, lax.rem(w + deep - k, deep))
        gather(x_gather, k, came, across)
        gather(s_gather, k, came, sibling)
    for k in range(deep):
        x_gather[k].wait_recv()
        came = place(c, 1 - x, lax.rem(w + deep - k, deep))
        gather(s_gather, deep + k, came, sibling)
    for k in range(2 * deep):
        s_gather[k].wait_recv()
    for store in (x_copies, z_copies, z_gather, x_gather, s_gather):
        sent += list(store.values())
    for one in sent:
        one.wait_send()


def body(deep, field, w_embed, embed_bias, w_query, w_key, w_value, w_out, latents, out_gain):
    tokens = field.shape[0]
    rows, width = latents.shape
    half, piece = rows // 2, rows // 4 // deep
    wide = width + 128
    copies = 1 + deep + (deep - 1) + (deep - 1) + deep + 2 * deep
    macs = tokens * width * width * 3 + rows * width * width + 2 * rows * tokens * width
    return pl.pallas_call(
        functools.partial(kernel, deep),
        out_shape=jax.ShapeDtypeStruct((rows, width), BF16),
        in_specs=[pl.BlockSpec(memory_space=pltpu.VMEM)] * 9,
        out_specs=pl.BlockSpec(memory_space=pltpu.VMEM),
        scratch_shapes=[
            pltpu.VMEM((rows, width), BF16),
            pltpu.VMEM((width, tokens), BF16),
            pltpu.VMEM((HEADS // 2, 2 * tokens, 256), BF16),
            pltpu.VMEM((128, 2 * width + 256), BF16),
            pltpu.VMEM((half, width), F32),
            pltpu.VMEM((half, 128), BF16),
            pltpu.VMEM((half, wide), BF16),
            pltpu.VMEM((half, wide), BF16),
            pltpu.VMEM((deep, piece, wide), BF16),
            pltpu.VMEM((deep, piece, wide), BF16),
            pltpu.VMEM((deep, piece, wide), BF16),
            pltpu.VMEM((deep, piece, wide), BF16),
            pltpu.SemaphoreType.DMA((copies,)),
            pltpu.SemaphoreType.DMA((copies,)),
        ],
        compiler_params=pltpu.CompilerParams(
            collective_id=0, has_side_effects=True, vmem_limit_bytes=48 * 2**20
        ),
        cost_estimate=pl.CostEstimate(
            flops=2 * macs, bytes_accessed=5 * 2**20, transcendentals=rows * tokens * HEADS
        ),
    )(
        field,
        w_embed,
        embed_bias.reshape(1, width),
        w_query,
        w_key,
        w_value,
        w_out,
        latents,
        out_gain.reshape(1, width),
    )


def solution(mesh):
    placed = (P(("group", "wide", "narrow"), None), P(), P(), P(), P(), P(), P(), P(), P())
    deep = mesh.shape["wide"]

    def pick(field, *rest):
        rows, width = rest[6].shape
        fits = mesh.shape["narrow"] == 4 and 2 <= deep <= 8 and rows % (64 * deep) == 0
        fits = fits and width == HEADS * 64 and field.shape[0] % 256 == 0
        return (functools.partial(body, deep) if fits else plain_body)(field, *rest)

    return jax.shard_map(
        pick, mesh=mesh, in_specs=placed, out_specs=P("group", None), check_vma=False
    )
```

time: 196 us -> 39.5 us (0.20)
  blocking collectives: 121 us -> 0 us
  Pallas kernels: 0 us -> 29.3 us
  waiting for transfers between devices: 25.4 us -> 0 us
  matrix products: 24.9 us -> 0 us
  between operations: 13.5 us -> 0.02 us
  other arithmetic: 8.88 us -> 0 us
  local copies, waits for them, and re-layouts: 2.6 us -> 9.63 us
    pmax x1 -> x0, blocking collectives: 62.9 us -> none  [body(): top = lax.pmax(local_top, ('wide', 'narrow'))]
    psum x1 -> x0, blocking collectives: 57.9 us -> none  [body(): numer_all, denom_all = lax.psum((numer, denom), ('wide', 'narrow'))]
    pallas_call x0 -> x1, Pallas kernels: none -> 29.3 us  [body(): pl.pallas_call(functools.partial(kernel, deep), out_shape=jax.ShapeDtypeS...]
    psum x1 -> x0, waiting for transfers between devices: 25.4 us -> none  [body(): numer_all, denom_all = lax.psum((numer, denom), ('wide', 'narrow'))]
    dot_general x9 -> x0, matrix products: 24.9 us -> none  [the longest x2 10.6 us: body(): jnp.einsum('lht,the->lhe', expo.astype(jnp.bfloat16), value_block, prefer...]
    unnamed x13 -> x19, local copies, waits for them, and re-layouts: 1.45 us -> 9.63 us
    reduce_sum x2 -> x0, other arithmetic: 7.37 us -> none  [the longest x1 7.19 us: body(): denom = denom + jnp.sum(expo, axis=2)]
  transfers between devices with their start and end apart: 1 -> 0, of which waited for: 1 -> 0; matrix products, arithmetic and copies ran while one was open for 4% -> 0% of each run, Pallas kernels for 0% -> 0%
where the time goes in v1:
time: 39.5 us; the launch traced here: 39 us
  Pallas kernels  29.3 us (74%)
  local copies, waits for them, and re-layouts  9.63 us (24%)
    pallas_call x1, Pallas kernels, body(): pl.pallas_call(functools.partial(kernel, deep), out_shape=jax.ShapeDtypeS...  29.3 us
    unnamed x19, local copies, waits for them, and re-layouts  9.63 us

profile of v1, /device:TPU:0, one launch (start us, length us, event | category | flops | bytes accessed | tf_op | source)
XLA Modules:
  0.0 39.0 jit_solution(9396790394309509731)
XLA Ops:
  0.0 0.0 copy-start.7
  0.0 0.7 %copy-done.7 = f32[512]{0:T(512)S(1)} copy-done((f32[512]{0:T(512)S(1)}, f32[512]{0:T(512)}, u32[]{:S(2)}) %copy-start.7) | copy-done | bytes 2072
  0.7 0.0 copy-start
  0.7 1.2 %copy-done = bf16[1024,512]{1,0:T(8,128)(2,1)S(1)} copy-done((bf16[1024,512]{1,0:T(8,128)(2,1)S(1)}, bf16[1024,512]{1,0:T(8,128)(2,1)}, u32[]{:S(2)}) %copy-start) | copy-done | bytes 1048600
  1.9 0.0 copy-start.1
  1.9 1.0 %copy-done.1 = bf16[512,512]{1,0:T(8,128)(2,1)S(1)} copy-done((bf16[512,512]{1,0:T(8,128)(2,1)S(1)}, bf16[512,512]{1,0:T(8,128)(2,1)}, u32[]{:S(2)}) %copy-start.1) | copy-done | bytes 524312
  3.0 0.0 copy-start.2
  3.0 1.0 %copy-done.2 = bf16[512,512]{1,0:T(8,128)(2,1)S(1)} copy-done((bf16[512,512]{1,0:T(8,128)(2,1)S(1)}, bf16[512,512]{1,0:T(8,128)(2,1)}, u32[]{:S(2)}) %copy-start.2) | copy-done | bytes 524312
  4.0 0.0 copy-start.3
  4.0 1.0 %copy-done.3 = bf16[512,512]{1,0:T(8,128)(2,1)S(1)} copy-done((bf16[512,512]{1,0:T(8,128)(2,1)S(1)}, bf16[512,512]{1,0:T(8,128)(2,1)}, u32[]{:S(2)}) %copy-start.3) | copy-done | bytes 524312
  5.0 0.0 copy-start.4
  5.0 1.0 %copy-done.4 = bf16[512,512]{1,0:T(8,128)(2,1)S(1)} copy-done((bf16[512,512]{1,0:T(8,128)(2,1)S(1)}, bf16[512,512]{1,0:T(8,128)(2,1)}, u32[]{:S(2)}) %copy-start.4) | copy-done | bytes 524312
  6.1 0.0 copy-start.5
  6.1 1.0 %copy-done.5 = bf16[512,512]{1,0:T(8,128)(2,1)S(1)} copy-done((bf16[512,512]{1,0:T(8,128)(2,1)S(1)}, bf16[512,512]{1,0:T(8,128)(2,1)}, u32[]{:S(2)}) %copy-start.5) | copy-done | bytes 524312
  7.1 0.0 copy-start.6
  7.1 1.0 %copy-done.6 = bf16[512,512]{1,0:T(8,128)(2,1)S(1)} copy-done((bf16[512,512]{1,0:T(8,128)(2,1)S(1)}, bf16[512,512]{1,0:T(8,128)(2,1)}, u32[]{:S(2)}) %copy-start.6) | copy-done | bytes 524312
  8.2 0.0 copy-start.8
  8.2 0.7 %copy-done.8 = f32[512]{0:T(512)S(1)} copy-done((f32[512]{0:T(512)S(1)}, f32[512]{0:T(512)}, u32[]{:S(2)}) %copy-start.8) | copy-done | bytes 2072
  8.8 29.3 %shard_map.91 = bf16[512,512]{1,0:T(8,128)(2,1)S(1)} custom-call(bf16[1024,512]{1,0:T(8,128)(2,1)S(1)} %copy-done, bf16[512,512]{1,0:T(8,128)(2,1)S(1)} %copy-done.1, f32[1,512]{1,0:T(1,128)S(1)} %bitcast.2, bf16[512,512]{1,0:T(8,128)(2,1)S(1)} %copy-done.2, bf16[512,512]{1,0:T(8,128)(2,1)S(1)} %copy-done.3, bf16[512,512]{1,0:T(8,128)(2,1)S(1)} %copy-done.4, ...), custom_call_target="tpu_custom_call" | custom-call | flops 2952790016 | bytes 5242880 | tf_op jit(solution)/shard_map/pallas_call | solution.py:304
  38.2 0.8 %copy.11 = bf16[512,512]{1,0:T(8,128)(2,1)} copy(bf16[512,512]{1,0:T(8,128)(2,1)S(1)} %shard_map.91) | data formatting | bytes 1048576
Async XLA Ops:
  0.0 0.7 %copy-start.7 = (f32[512]{0:T(512)S(1)}, f32[512]{0:T(512)}, u32[]{:S(2)}) copy-start(f32[512]{0:T(512)} %param.11) | copy-start | bytes 6148
  0.7 1.2 %copy-start = (bf16[1024,512]{1,0:T(8,128)(2,1)S(1)}, bf16[1024,512]{1,0:T(8,128)(2,1)}, u32[]{:S(2)}) copy-start(bf16[1024,512]{1,0:T(8,128)(2,1)} %field.1) | copy-start | bytes 3145732
  1.9 1.0 %copy-start.1 = (bf16[512,512]{1,0:T(8,128)(2,1)S(1)}, bf16[512,512]{1,0:T(8,128)(2,1)}, u32[]{:S(2)}) copy-start(bf16[512,512]{1,0:T(8,128)(2,1)} %w_embed.1) | copy-start | bytes 1572868
  3.0 1.0 %copy-start.2 = (bf16[512,512]{1,0:T(8,128)(2,1)S(1)}, bf16[512,512]{1,0:T(8,128)(2,1)}, u32[]{:S(2)}) copy-start(bf16[512,512]{1,0:T(8,128)(2,1)} %w_query.1) | copy-start | bytes 1572868
  4.0 1.0 %copy-start.3 = (bf16[512,512]{1,0:T(8,128)(2,1)S(1)}, bf16[512,512]{1,0:T(8,128)(2,1)}, u32[]{:S(2)}) copy-start(bf16[512,512]{1,0:T(8,128)(2,1)} %w_key.1) | copy-start | bytes 1572868
  5.0 1.0 %copy-start.4 = (bf16[512,512]{1,0:T(8,128)(2,1)S(1)}, bf16[512,512]{1,0:T(8,128)(2,1)}, u32[]{:S(2)}) copy-start(bf16[512,512]{1,0:T(8,128)(2,1)} %w_value.1) | copy-start | bytes 1572868
  6.1 1.0 %copy-start.5 = (bf16[512,512]{1,0:T(8,128)(2,1)S(1)}, bf16[512,512]{1,0:T(8,128)(2,1)}, u32[]{:S(2)}) copy-start(bf16[512,512]{1,0:T(8,128)(2,1)} %w_out.1) | copy-start | bytes 1572868
  7.1 1.0 %copy-start.6 = (bf16[512,512]{1,0:T(8,128)(2,1)S(1)}, bf16[512,512]{1,0:T(8,128)(2,1)}, u32[]{:S(2)}) copy-start(bf16[512,512]{1,0:T(8,128)(2,1)} %latents.1) | copy-start | bytes 1572868
  8.2 0.7 %copy-start.8 = (f32[512]{0:T(512)S(1)}, f32[512]{0:T(512)}, u32[]{:S(2)}) copy-start(f32[512]{0:T(512)} %param.17) | copy-start | bytes 6148

commit v2 on v1

--- a/solution.py
+++ b/solution.py
@@ -103,6 +103,35 @@
 
 def kernel(
     deep,
+    *refs,
+):
+    sources, out, held = refs[:9], refs[9], refs[10:19]
+    field, w_embed, embed_bias, w_query, w_key, w_value, w_out, latents, out_gain = held
+    load = refs[-1]
+    compute(deep, Loads(sources, held, load), *held, out, *refs[19:-1])
+
+
+class Loads:
+    ORDER = (7, 3, 0, 1, 2, 4, 5, 6, 8)
+
+    def __init__(self, sources, held, load):
+        self.copies = [
+            pltpu.make_async_copy(source, target, load.at[i])
+            for i, (source, target) in enumerate(zip(sources, held))
+        ]
+
+    def start(self):
+        for i in self.ORDER:
+            self.copies[i].start()
+
+    def wait(self, *which):
+        for i in which:
+            self.copies[i].wait()
+
+
+def compute(
+    deep,
+    loads,
     field,
     w_embed,
     embed_bias,
@@ -125,6 +154,8 @@
     x_in,
     z_out,
     z_in,
+    mine_numer,
+    mine_stat,
     send,
     recv,
 ):
@@ -134,6 +165,7 @@
     head_dim = width // heads
     half, quarter, piece = rows // 2, rows // 4, rows // 4 // deep
 
+    loads.start()
     group, w, n = lax.axis_index("group"), lax.axis_index("wide"), lax.axis_index("narrow")
     c, x = lax.rem(n, 2), n // 2
     sibling = (group, w, x * 2 + 1 - c)
@@ -155,11 +187,13 @@
         )
 
     make_spread(spread, width, heads)
+    loads.wait(3, 7)
     queries[...] = (
         jnp.dot(latents[...], w_query[...], preferred_element_type=F32) * head_dim ** (-0.5)
     ).astype(BF16)
 
     chunk = 256
+    loads.wait(0, 1, 2, 4, 5)
 
     @pl.loop(0, tokens // chunk)
     def project(step):
@@ -212,10 +246,10 @@
     sent[0].wait_recv()
 
     def chip_sum(at):
-        at = pl.multiple_of(at, piece)
+        at = pl.multiple_of(at, quarter)
         return merge(
-            [own_numer[pl.ds(at, piece), :], core_in[pl.ds(at, piece), :width]],
-            [own_stat[pl.ds(at, piece), :], core_in[pl.ds(at, piece), width:]],
+            [own_numer[pl.ds(at, quarter), :], core_in[pl.ds(at, quarter), :width]],
+            [own_stat[pl.ds(at, quarter), :], core_in[pl.ds(at, quarter), width:]],
             spread,
             width,
         )
@@ -223,18 +257,21 @@
     order = list(range(1, deep)) + [0]
     index = 1
     x_copies = {}
+    x_numer, x_stat = chip_sum((1 - x) * quarter)
+    x_out[:, :width] = x_numer.astype(BF16)
+    x_out[:, width:] = x_stat
     for k in order:
-        block = lax.rem(w + k, deep)
-        numer, stat = chip_sum((1 - x) * quarter + block * piece)
-        x_out[k, :, :width] = numer.astype(BF16)
-        x_out[k, :, width:] = stat
-        x_copies[k] = copy(index, x_out.at[k], x_in.at[k], across)
+        block = pl.ds(pl.multiple_of(lax.rem(w + k, deep) * piece, piece), piece)
+        x_copies[k] = copy(index, x_out.at[block], x_in.at[k], across)
         x_copies[k].start()
         index += 1
+    x_numer, x_stat = chip_sum(x * quarter)
+    mine_numer[...] = x_numer
+    mine_stat[...] = x_stat
     mine = {}
     for k in order:
-        block = lax.rem(w + k, deep)
-        mine[k] = chip_sum(x * quarter + block * piece)
+        block = pl.ds(pl.multiple_of(lax.rem(w + k, deep) * piece, piece), piece)
+        mine[k] = (mine_numer[block, :], mine_stat[block, :])
     z_copies = {}
     for k in order:
         x_copies[k].wait_recv()
@@ -258,6 +295,7 @@
         return pl.ds(pl.multiple_of(core * half + column * quarter + slab * piece, piece), piece)
 
     own = place(c, x, w)
+    loads.wait(6, 8)
     mixed = latents[own, :].astype(F32) + jnp.dot(
         attended, w_out[...], preferred_element_type=F32
     )
@@ -277,15 +315,20 @@
         gather(z_gather, k, own, along[k])
     gather(x_gather, 0, own, across)
     gather(s_gather, 0, own, sibling)
+
+    def relay(k):
+        x_gather[k].wait_recv()
+        gather(s_gather, deep + k, place(c, 1 - x, lax.rem(w + deep - k, deep)), sibling)
+
     for k in range(1, deep):
         z_gather[k].wait_recv()
         came = place(c, x, lax.rem(w + deep - k, deep))
         gather(x_gather, k, came, across)
         gather(s_gather, k, came, sibling)
-    for k in range(deep):
-        x_gather[k].wait_recv()
-        came = place(c, 1 - x, lax.rem(w + deep - k, deep))
-        gather(s_gather, deep + k, came, sibling)
+        if k > 1:
+            relay(k - 2)
+    relay(deep - 2)
+    relay(deep - 1)
     for k in range(2 * deep):
         s_gather[k].wait_recv()
     for store in (x_copies, z_copies, z_gather, x_gather, s_gather):
@@ -299,36 +342,7 @@
     rows, width = latents.shape
     half, piece = rows // 2, rows // 4 // deep
     wide = width + 128
-    copies = 1 + deep + (deep - 1) + (deep - 1) + deep + 2 * deep
-    macs = tokens * width * width * 3 + rows * width * width + 2 * rows * tokens * width
-    return pl.pallas_call(
-        functools.partial(kernel, deep),
-        out_shape=jax.ShapeDtypeStruct((rows, width), BF16),
-        in_specs=[pl.BlockSpec(memory_space=pltpu.VMEM)] * 9,
-        out_specs=pl.BlockSpec(memory_space=pltpu.VMEM),
-        scratch_shapes=[
-            pltpu.VMEM((rows, width), BF16),
-            pltpu.VMEM((width, tokens), BF16),
-            pltpu.VMEM((HEADS // 2, 2 * tokens, 256), BF16),
-            pltpu.VMEM((128, 2 * width + 256), BF16),
-            pltpu.VMEM((half, width), F32),
-            pltpu.VMEM((half, 128), BF16),
-            pltpu.VMEM((half, wide), BF16),
-            pltpu.VMEM((half, wide), BF16),
-            pltpu.VMEM((deep, piece, wide), BF16),
-            pltpu.VMEM((deep, piece, wide), BF16),
-            pltpu.VMEM((deep, piece, wide), BF16),
-            pltpu.VMEM((deep, piece, wide), BF16),
-            pltpu.SemaphoreType.DMA((copies,)),
-            pltpu.SemaphoreType.DMA((copies,)),
-        ],
-        compiler_params=pltpu.CompilerParams(
-            collective_id=0, has_side_effects=True, vmem_limit_bytes=48 * 2**20
-        ),
-        cost_estimate=pl.CostEstimate(
-            flops=2 * macs, bytes_accessed=5 * 2**20, transcendentals=rows * tokens * HEADS
-        ),
-    )(
+    arguments = (
         field,
         w_embed,
         embed_bias.reshape(1, width),
@@ -339,6 +353,40 @@
         latents,
         out_gain.reshape(1, width),
     )
+    copies = 1 + deep + (deep - 1) + (deep - 1) + deep + 2 * deep
+    macs = tokens * width * width * 3 + rows * width * width + 2 * rows * tokens * width
+    return pl.pallas_call(
+        functools.partial(kernel, deep),
+        out_shape=jax.ShapeDtypeStruct((rows, width), BF16),
+        in_specs=[pl.BlockSpec(memory_space=pltpu.HBM)] * 9,
+        out_specs=pl.BlockSpec(memory_space=pltpu.VMEM),
+        scratch_shapes=[pltpu.VMEM(a.shape, a.dtype) for a in arguments]
+        + [
+            pltpu.VMEM((rows, width), BF16),
+            pltpu.VMEM((width, tokens), BF16),
+            pltpu.VMEM((HEADS // 2, 2 * tokens, 256), BF16),
+            pltpu.VMEM((128, 2 * width + 256), BF16),
+            pltpu.VMEM((half, width), F32),
+            pltpu.VMEM((half, 128), BF16),
+            pltpu.VMEM((half, wide), BF16),
+            pltpu.VMEM((half, wide), BF16),
+            pltpu.VMEM((rows // 4, wide), BF16),
+            pltpu.VMEM((deep, piece, wide), BF16),
+            pltpu.VMEM((deep, piece, wide), BF16),
+            pltpu.VMEM((deep, piece, wide), BF16),
+            pltpu.VMEM((rows // 4, width), F32),
+            pltpu.VMEM((rows // 4, 128), BF16),
+            pltpu.SemaphoreType.DMA((copies,)),
+            pltpu.SemaphoreType.DMA((copies,)),
+            pltpu.SemaphoreType.DMA((9,)),
+        ],
+        compiler_params=pltpu.CompilerParams(
+            collective_id=0, has_side_effects=True, vmem_limit_bytes=63 * 2**20
+        ),
+        cost_estimate=pl.CostEstimate(
+            flops=2 * macs, bytes_accessed=5 * 2**20, transcendentals=rows * tokens * HEADS
+        ),
+    )(*arguments)
 
 
 def solution(mesh):

time: 39.5 us -> 34.2 us (0.87)
  local copies, waits for them, and re-layouts: 9.63 us -> 1.87 us
  Pallas kernels: 29.3 us -> 32.1 us
    unnamed x19 -> x1, local copies, waits for them, and re-layouts: 9.63 us -> 1.87 us
    pallas_call x1, Pallas kernels: 29.3 us -> 32.1 us  [body(): pl.pallas_call(functools.partial(kernel, deep), out_shape=jax.ShapeDtypeS...]
where the time goes in v2:
time: 34.2 us; the launch traced here: 34 us
  Pallas kernels  32.1 us (94%)
  local copies, waits for them, and re-layouts  1.87 us (5%)
    pallas_call x1, Pallas kernels, body(): pl.pallas_call(functools.partial(kernel, deep), out_shape=jax.ShapeDtypeS...  32.1 us
    unnamed x1, local copies, waits for them, and re-layouts  1.87 us

profile of v2, /device:TPU:0, one launch (start us, length us, event | category | flops | bytes accessed | tf_op | source)
XLA Modules:
  0.0 34.0 jit_solution(7930314311174083244)
XLA Ops:
  0.0 32.1 %shard_map.91 = bf16[512,512]{1,0:T(8,128)(2,1)} custom-call(bf16[1024,512]{1,0:T(8,128)(2,1)} %refs_0_.1, bf16[512,512]{1,0:T(8,128)(2,1)} %refs_1_.1, f32[1,512]{1,0:T(1,128)} %bitcast.2, bf16[512,512]{1,0:T(8,128)(2,1)} %refs_3_.1, bf16[512,512]{1,0:T(8,128)(2,1)} %refs_4_.1, bf16[512,512]{1,0:T(8,128)(2,1)} %refs_5_.1, bf16[512,512]{1,0:T(8,128)(2,1)} %refs_6_.1, ...), custom_call_target="tpu_custom_call" | custom-call | flops 2952790016 | bytes 5242880 | tf_op jit(solution)/shard_map/pallas_call | solution.py:358
  32.2 1.9 %copy.11 = bf16[512,512]{1,0:T(8,128)(2,1)} copy(bf16[512,512]{1,0:T(8,128)(2,1)} %shard_map.91) | data formatting | bytes 1048576

commit v3 on v2

--- a/solution.py
+++ b/solution.py
@@ -381,12 +381,12 @@
             pltpu.SemaphoreType.DMA((9,)),
         ],
         compiler_params=pltpu.CompilerParams(
-            collective_id=0, has_side_effects=True, vmem_limit_bytes=63 * 2**20
+            collective_id=0, has_side_effects=True, vmem_limit_bytes=40 * 2**20
         ),
         cost_estimate=pl.CostEstimate(
             flops=2 * macs, bytes_accessed=5 * 2**20, transcendentals=rows * tokens * HEADS
         ),
-    )(*arguments)
+    )(*[pltpu.with_memory_space_constraint(a, pltpu.HBM) for a in arguments])
 
 
 def solution(mesh):

time: 34.2 us -> 32.3 us (0.944)
  local copies, waits for them, and re-layouts: 1.87 us -> 0.8 us
  Pallas kernels: 32.1 us -> 31.4 us
    unnamed x1, local copies, waits for them, and re-layouts: 1.87 us -> 0.8 us
    pallas_call x1, Pallas kernels: 32.1 us -> 31.4 us  [body(): pl.pallas_call(functools.partial(kernel, deep), out_shape=jax.ShapeDtypeS...]
where the time goes in v3:
time: 32.3 us; the launch traced here: 32.2 us
  Pallas kernels  31.4 us (97%)
  local copies, waits for them, and re-layouts  0.8 us (2%)
    pallas_call x1, Pallas kernels, body(): pl.pallas_call(functools.partial(kernel, deep), out_shape=jax.ShapeDtypeS...  31.4 us
    unnamed x1, local copies, waits for them, and re-layouts  0.8 us

profile of v3, /device:TPU:0, one launch (start us, length us, event | category | flops | bytes accessed | tf_op | source)
XLA Modules:
  0.0 32.2 jit_solution(13996290031009155332)
XLA Ops:
  0.0 31.4 %shard_map.91 = bf16[512,512]{1,0:T(8,128)(2,1)S(1)} custom-call(bf16[1024,512]{1,0:T(8,128)(2,1)} %refs_0_.1, bf16[512,512]{1,0:T(8,128)(2,1)} %refs_1_.1, f32[1,512]{1,0:T(1,128)} %bitcast.2, bf16[512,512]{1,0:T(8,128)(2,1)} %refs_3_.1, bf16[512,512]{1,0:T(8,128)(2,1)} %refs_4_.1, bf16[512,512]{1,0:T(8,128)(2,1)} %refs_5_.1, bf16[512,512]{1,0:T(8,128)(2,1)} %refs_6_.1, ...), custom_call_target="tpu_custom_call" | custom-call | flops 2952790016 | bytes 5242880 | tf_op jit(solution)/shard_map/pallas_call | solution.py:358
  31.4 0.8 %copy.11 = bf16[512,512]{1,0:T(8,128)(2,1)} copy(bf16[512,512]{1,0:T(8,128)(2,1)S(1)} %shard_map.91) | data formatting | bytes 1048576
